TPU v7x, 32 devices: a whole 2x2x4 slice. The times are simulated.
32 devices in a mesh: grp: 2 (over core), dev: 16 (over z, y, x).
Axes of the slice: x: 2, y: 2, z: 4, core: 2. Of those that a mesh axis runs over, the one named last changes fastest.
Arguments:
- centres: bfloat16 [65536, 512], P(('grp', 'dev')), may hold values from -12 to 12
- coefficients: float32 [100, 65536], P(None, ('grp', 'dev')), may hold values from -0.25 to 0.25
- targets: float32 [100, 512], P(None, ('grp', 'dev')), may hold values from -6 to 6
- batch_index: int32 [512], P(('grp', 'dev')), may hold values from 0 to 2047
- nys_index: int32 [512], P(('grp', 'dev')), may hold values from 0 to 2047
- eigvecs: float32 [512, 128], P(('grp', 'dev')), may hold values from -0.25 to 0.25
- eig_scale: float32 [128], replicated, may hold values from 0.1 to 2
Outputs:
- updated: float32 [100, 65536], P(None, ('grp', 'dev'))
- residual: float32 [100, 512], P(None, ('grp', 'dev'))
Inputs may be any that keep to these rules, and one draw needn't show every extreme that they name: `batch_index`: entries of the k-th block of 16 name rows within the k-th block of 2048 centres. `nys_index`: entries of the k-th block of 16 name rows within the k-th block of 2048 centres.
All inputs are finite; a program needn't handle non-finite values.
Results may differ from a plain program's by a relative error of at most 0.0031.
Values may be sent and summed in bfloat16 or wider, within the bound.
A program may use at most 64 MiB of HBM per device.

v0:
```python
import math

import jax
import jax.numpy as jnp
from jax import lax
from jax.sharding import PartitionSpec as P

step_rate = 1.0


def kernel_block(left_rows, right_rows, spread):
    left_sq = jnp.sum(jnp.square(left_rows.astype(jnp.float32)), axis=1)
    right_sq = jnp.sum(jnp.square(right_rows.astype(jnp.float32)), axis=1)
    cross_dot = lax.dot_general(
        left_rows, right_rows, (((1,), (1,)), ((), ())), preferred_element_type=jnp.float32
    )
    distance = jnp.sqrt(jnp.maximum(left_sq[:, None] + right_sq[None, :] - 2.0 * cross_dot, 1.0))
    return jnp.exp(-distance / spread)


def per_device(centres, coefficients, targets, batch_index, nys_index, eigvecs, eig_scale):
    own_centres, feature_dim = centres.shape
    outputs = coefficients.shape[0]
    own_batch = targets.shape[1]
    spread = 0.7 * math.sqrt(feature_dim)
    columns = lax.iota(jnp.int32, own_centres)
    batch_pick = batch_index[:, None] == columns[None, :]
    nys_pick = nys_index[:, None] == columns[None, :]
    own_rows = jnp.dot(
        batch_pick.astype(jnp.bfloat16), centres, preferred_element_type=jnp.float32
    ).astype(jnp.bfloat16)
    nys_rows = jnp.dot(
        nys_pick.astype(jnp.bfloat16), centres, preferred_element_type=jnp.float32
    ).astype(jnp.bfloat16)
    coef_bf = coefficients.astype(jnp.bfloat16)

    def score_block(batch_piece):
        kernel = kernel_block(batch_piece, centres, spread).astype(jnp.bfloat16)
        partial_value = lax.dot_general(
            coef_bf, kernel, (((1,), (1,)), ((), ())), preferred_element_type=jnp.float32
        )
        nys_kernel = kernel_block(nys_rows, batch_piece, spread)
        return jnp.concatenate([partial_value, nys_kernel], axis=0)

    def score(batch_piece):
        row_count = batch_piece.shape[0]
        if row_count > 512 and row_count % 512 == 0:
            blocks = batch_piece.reshape(row_count // 512, 512, feature_dim)
            stacked_blocks = lax.map(score_block, blocks)
            return jnp.transpose(stacked_blocks, (1, 0, 2)).reshape(
                stacked_blocks.shape[1], row_count
            )
        return score_block(batch_piece)

    stacked = score(lax.all_gather(own_rows, ("grp", "dev"), axis=0, tiled=True))
    partial_value = stacked[:outputs]
    nys_kernel = stacked[outputs:]
    position = lax.axis_index(("grp", "dev")) * own_batch
    basis_part = lax.dot_general(
        eigvecs, nys_kernel, (((0,), (0,)), ((), ())), precision=lax.Precision.HIGHEST
    )
    basis_total = lax.psum(basis_part, ("grp", "dev"))
    own_part = lax.dynamic_slice_in_dim(partial_value, position, own_batch, 1)
    partial_value = lax.dynamic_update_slice_in_dim(partial_value, own_part - targets, position, 1)
    residual = lax.psum(partial_value, ("grp", "dev"))
    residual_own = lax.dynamic_slice_in_dim(residual, position, own_batch, 1)
    projected = lax.dot_general(
        basis_total, residual, (((1,), (1,)), ((), ())), precision=lax.Precision.HIGHEST
    )
    correction = jnp.dot(eigvecs, eig_scale[:, None] * projected, precision=lax.Precision.HIGHEST)
    batch_change = lax.dot_general(
        residual_own,
        batch_pick.astype(jnp.float32),
        (((1,), (0,)), ((), ())),
        precision=lax.Precision.HIGHEST,
    )
    nys_change = lax.dot_general(
        correction,
        nys_pick.astype(jnp.float32),
        (((0,), (0,)), ((), ())),
        precision=lax.Precision.HIGHEST,
    )
    updated = coefficients - step_rate * batch_change + step_rate * nys_change
    return (updated, residual_own)


def solution(mesh):
    in_specs = (
        P(("grp", "dev"), None),
        P(None, ("grp", "dev")),
        P(None, ("grp", "dev")),
        P(("grp", "dev")),
        P(("grp", "dev")),
        P(("grp", "dev"), None),
        P(),
    )
    out_specs = (P(None, ("grp", "dev")), P(None, ("grp", "dev")))
    return jax.shard_map(
        per_device, mesh=mesh, in_specs=in_specs, out_specs=out_specs, check_vma=False
    )
```

profile of v0, /device:TPU:0, one launch (start us, length us, event | category | flops | bytes accessed | tf_op | source)
XLA Modules:
  0.0 231.6 jit_solution(1346905743815812533)
XLA Ops:
  7.2 0.0 copy-start
  7.2 0.0 copy-start.1
  7.2 0.0 all-reduce.3.cloned.1.call-start
  7.3 0.0 copy-start.6
  7.3 2.8 %multiply_reduce_fusion = f32[2048]{0:T(1024)} fusion(bf16[2048,512]{1,0:T(8,128)(2,1)} %param.7), kind=kLoop, calls=%fused_computation.1 | loop fusion | flops 3143680 | bytes 2105344 | tf_op jit(solution)/shard_map/reduce_sum | solution.py:13
  10.1 0.4 convolution_convert_fusion.1
  10.5 0.0 copy-start.2
  10.5 1.6 multiply_reduce_fusion.2
  12.2 0.1 copy.9
  12.3 72.9 %all_gather.3 = bf16[512,512]{1,0:T(8,128)(2,1)S(1)} all-gather(bf16[16,512]{1,0:T(8,128)(2,1)S(1)} %convolution_convert_fusion.1), channel_id=1, replica_groups=mesh['grp'=2,'dev'=16] {'grp','dev'}, dimensions={0}, use_global_device_ids=true | all-gather | bytes 540672 | tf_op jit(solution)/shard_map/all_gather | solution.py:55
  85.2 0.2 multiply_reduce_fusion.1
  85.4 1.6 fusion.6
  87.0 4.2 %fusion = f32[512,100]{0,1:T(8,128)} fusion(bf16[512,512]{1,0:T(8,128)(2,1)S(1)} %all_gather.3, bf16[2048,512]{1,0:T(8,128)(2,1)S(1)} %copy-done.1, f32[2048]{0:T(1024)} %multiply_reduce_fusion, f32[512]{0:T(512)S(1)} %multiply_reduce_fusion.1, f32[100,2048]{1,0:T(8,128)S(1)} %copy-done.2), kind=kOutput, calls=%fused_computation.4 | convolution fusion | flops 1291001856 | bytes 3655680 | tf_op jit(solution)/shard_map/dot_general | solution.py:39
  91.2 0.9 bitcast_subtract_fusion
  92.1 1.5 dynamic_update_slice.3
  93.6 2.1 convolution_bitcast_fusion
  95.7 0.0 all-reduce.3.cloned.1.call-update
  95.7 123.5 %all-reduce.3.cloned.1.call-done = (f32[100,512]{1,0:T(8,128)}, f32[128,512]{0,1:T(8,128)}) async-done(((f32[100,512]{1,0:T(8,128)}, f32[128,512]{0,1:T(8,128)}), (f32[100,512]{1,0:T(8,128)}, f32[128,512]{0,1:T(8,128)})) %all-reduce.3.cloned.1.call-update) | async-done | bytes 466960 | tf_op jit(solution)/shard_map/psum | solution.py:65
  219.2 0.9 constant_dynamic-slice_fusion
  220.1 0.7 copy.10
  220.8 0.6 convolution_subtract_fusion
  221.4 1.5 convolution_multiply_fusion
  222.9 0.3 fusion.15
  223.2 1.5 convolution_add_fusion
  (14 shorter events, 0.0 us)
Async XLA Ops:
  7.2 86.5 %copy-start = (f32[16,128]{1,0:T(8,128)S(1)}, f32[16,128]{1,0:T(8,128)}, u32[]{:S(2)}) copy-start(f32[16,128]{1,0:T(8,128)} %param.12) | copy-start | bytes 24580
  7.2 2.9 %copy-start.1 = (bf16[2048,512]{1,0:T(8,128)(2,1)S(1)}, bf16[2048,512]{1,0:T(8,128)(2,1)}, u32[]{:S(2)}) copy-start(bf16[2048,512]{1,0:T(8,128)(2,1)} %param.7) | copy-start | bytes 6291460
  7.2 2.9 %copy-start.5 = (s32[16]{0:T(128)S(1)}, s32[16]{0:T(128)}, u32[]{:S(2)}) copy-start(s32[16]{0:T(128)} %param.10) | copy-start | bytes 196
  7.2 212.0 %all-reduce.3.cloned.1.call-start = ((), (), s32[]{:S(2)}) async-start(), calls=%async_computation | async-start | bytes 950272 | tf_op jit(solution)/shard_map/psum | solution.py:65
  7.3 3.2 %copy-start.6 = (s32[16]{0:T(128)S(1)}, s32[16]{0:T(128)}, u32[]{:S(2)}) copy-start(s32[16]{0:T(128)} %param.11) | copy-start | bytes 196
  10.1 2.1 copy-start.4
  10.5 76.5 %copy-start.2 = (f32[100,2048]{1,0:T(8,128)S(1)}, f32[100,2048]{1,0:T(8,128)}, u32[]{:S(2)}) copy-start(f32[100,2048]{1,0:T(8,128)} %param.8) | copy-start | bytes 2457604
  91.2 130.2 %copy-start.8 = (f32[128]{0:T(128)S(1)}, f32[128]{0:T(128)}, u32[]{:S(2)}) copy-start(f32[128]{0:T(128)} %param.13) | copy-start | bytes 1540
  91.2 132.0 %copy-start.7 = (s32[16]{0:T(128)S(1)}, s32[16]{0:T(128)}, u32[]{:S(2)}) copy-start(s32[16]{0:T(128)} %param.11) | copy-start | bytes 196
  219.2 2.2 copy-start.3
Sparse Core Ops, SparseCore 0:
  95.8 123.2 all-reduce.2
where the time goes:
time: 232 us
  waiting for transfers between devices  123 us (53%)
  blocking collectives  72.9 us (31%)
  between operations  14.1 us (6%)
  matrix products  13.8 us (6%)
  other arithmetic  3.89 us (2%)
  local copies, waits for them, and re-layouts  3.28 us (1%)
    psum x1, waiting for transfers between devices, per_device(): residual = lax.psum(partial_value, ('grp', 'dev'))  123 us
    all_gather x1, blocking collectives, per_device(): lax.all_gather(own_rows, ('grp', 'dev'), axis=0, tiled=True)  72.9 us
  transfers between devices with their start and end apart: 1, of which 1 were waited for; matrix products, arithmetic and copies ran while one was open for 0% of the time, Pallas kernels for 0%

commit v1 on v0

v1 whole, which is shorter than its diff:
```python
import functools
import math

import jax
import jax.numpy as jnp
from jax import lax
from jax.experimental import pallas as pl
from jax.experimental.pallas import tpu as pltpu
from jax.sharding import PartitionSpec as P

MESH = pl.DeviceIdType.MESH
HIGHEST = lax.Precision.HIGHEST
NN = (((1,), (0,)), ((), ()))
NT = (((1,), (1,)), ((), ()))
TN = (((0,), (0,)), ((), ()))


def mm(a, b, dims=NN, precision=None):
    return lax.dot_general(a, b, dims, precision=precision, preferred_element_type=jnp.float32)


def split_square(x):
    f = x.astype(jnp.float32)
    f = f * f
    high = f.astype(jnp.bfloat16)
    low = (f - high.astype(jnp.float32)).astype(jnp.bfloat16)
    return high, low


def square_column(x):
    high, low = split_square(x)
    ones = jnp.ones((x.shape[1], 128), jnp.bfloat16)
    return mm(high, ones) + mm(low, ones)


def square_row(x):
    high, low = split_square(x)
    ones = jnp.ones((8, x.shape[1]), jnp.bfloat16)
    return (mm(ones, high, NT) + mm(ones, low, NT))[0:1]


def laplace(left, left_sq, minus_two_right, right_sq, rate):
    cross = mm(left, minus_two_right, NT)
    wide = jnp.concatenate([left_sq] * (cross.shape[1] // 128), axis=1)
    d2 = jnp.maximum((wide + right_sq) + cross, 1.0)
    return jnp.exp2((d2 * lax.rsqrt(d2)) * rate)


def kernel(n_grp, n_dev, bidx, nidx, scale, targets, eig, centres_hbm, coef_hbm,
           updated, res_out,
           centres, coef, coef_bf, csq, rows, nys, eigs, pick, acc, part, got, res, gain, square,
           local_sem, send_sem, recv_sem):
    n = n_grp * n_dev
    grp, dev = lax.axis_index("grp"), lax.axis_index("dev")
    me = grp * n_dev + dev
    c_dev, feat = centres.shape
    outs = coef.shape[0]
    b_dev, s_dev = bidx.shape[0], nidx.shape[0]
    batch, sub = rows.shape[0], nys.shape[0]
    rate = -1.0 / (0.7 * math.sqrt(feat) * math.log(2.0))
    wide_out = part.shape[1]

    load_centres = pltpu.make_async_copy(centres_hbm, centres, local_sem.at[0])
    load_coef = pltpu.make_async_copy(coef_hbm, coef, local_sem.at[1])
    load_centres.start()
    load_coef.start()

    def peer_id(k):
        p = lax.rem(me + k, n)
        return p, {"grp": p // n_dev, "dev": lax.rem(p, n_dev)}

    barrier = pltpu.get_barrier_semaphore()

    @pl.loop(1, n)
    def _(k):
        _, where = peer_id(k)
        pl.semaphore_signal(barrier, inc=1, device_id=where, device_id_type=MESH)

    def block(ref, p, size):
        return ref.at[pl.ds(pl.multiple_of(p * size, size), size)]

    def send_all(src, dst, size, slot, gather):
        @pl.loop(1, n)
        def _(k):
            p, where = peer_id(k)
            pltpu.make_async_remote_copy(
                src_ref=block(src, me if gather else p, size), dst_ref=block(dst, me, size),
                send_sem=send_sem.at[slot], recv_sem=recv_sem.at[slot],
                device_id=where, device_id_type=MESH).start()

    def all_but_one(ref, size, slot):
        piece = ref.at[pl.ds(0, (n - 1) * size)]
        _, where = peer_id(1)
        return pltpu.make_async_remote_copy(
            src_ref=piece, dst_ref=piece, send_sem=send_sem.at[slot], recv_sem=recv_sem.at[slot],
            device_id=where, device_id_type=MESH)

    total = b_dev + s_dev
    spot = lax.broadcasted_iota(jnp.int32, (total, 128), 0)
    index = jnp.zeros((total, 128), jnp.int32)
    for r in range(b_dev):
        index = jnp.where(spot == r, bidx[r], index)
    for r in range(s_dev):
        index = jnp.where(spot == b_dev + r, nidx[r], index)
    index = jnp.concatenate([index] * (c_dev // 128), axis=1)
    hit = lax.broadcasted_iota(jnp.int32, (total, c_dev), 1) == index
    pick[...] = jnp.where(hit, 1.0, 0.0).astype(jnp.bfloat16)

    load_centres.wait()
    own = mm(pick[...], centres[...]).astype(jnp.bfloat16)
    block(rows, me, b_dev)[...] = own[:b_dev]
    block(nys, me, s_dev)[...] = own[b_dev:]
    block(eigs, me, s_dev)[...] = eig[...]

    pl.semaphore_wait(barrier, n - 1)
    send_all(rows, rows, b_dev, 0, True)
    send_all(nys, nys, s_dev, 1, True)
    send_all(eigs, eigs, s_dev, 2, True)

    step = 256 if c_dev % 256 == 0 else 128

    @pl.loop(0, c_dev // step)
    def _(i):
        piece = pl.ds(pl.multiple_of(i * step, step), step)
        csq[piece, :] = square_column(centres[piece, :])

    load_coef.wait()
    coef_bf[...] = coef[...].astype(jnp.bfloat16)
    square[...] = jnp.zeros_like(square)
    square[0:outs, 0:b_dev] = targets[...]
    target = jnp.transpose(square[...])[0:b_dev]
    acc[...] = jnp.zeros_like(acc)

    width = acc.shape[1]
    all_but_one(rows, b_dev, 0).wait_recv()

    @pl.loop(0, batch // width)
    def _(j):
        across = pl.ds(pl.multiple_of(j * width, width), width)
        piece_rows = rows[across, :]
        bsq = square_row(piece_rows)
        minus_two = piece_rows * jnp.bfloat16(-2.0)
        sums = jnp.zeros((outs, width), jnp.float32)
        for i in range(c_dev // step):
            down = slice(i * step, (i + 1) * step)
            k = laplace(centres[down, :], csq[down, :], minus_two, bsq, rate).astype(jnp.bfloat16)
            sums = sums + mm(coef_bf[:, down], k)
        acc[0:outs, :] = sums
        part[across, :] = jnp.transpose(acc[...])

    send_all(part, got, b_dev, 3, False)
    block(got, me, b_dev)[...] = block(part, me, b_dev)[...]

    all_but_one(nys, s_dev, 1).wait_recv()
    all_but_one(eigs, s_dev, 2).wait_recv()
    weights = mm(eig[...] * scale[...], eigs[...], NT, HIGHEST)
    tall = min(512, sub)

    @pl.loop(0, batch // width)
    def _(j):
        across = pl.ds(pl.multiple_of(j * width, width), width)
        piece_rows = rows[across, :]
        bsq = square_row(piece_rows)
        minus_two = piece_rows * jnp.bfloat16(-2.0)
        total_gain = jnp.zeros((s_dev, width), jnp.float32)
        for i in range(sub // tall):
            piece_nys = nys[i * tall:(i + 1) * tall, :]
            kn = laplace(piece_nys, square_column(piece_nys), minus_two, bsq, rate)
            total_gain = total_gain + mm(weights[:, i * tall:(i + 1) * tall], kn, NN, HIGHEST)
        gain[:, across] = total_gain

    all_but_one(got, b_dev, 3).wait_recv()
    own_res = jnp.sum(got[...].reshape(n, b_dev, wide_out), axis=0) - target
    block(res, me, b_dev)[...] = own_res
    send_all(res, res, b_dev, 4, True)
    square[0:b_dev, :] = own_res
    res_out[...] = jnp.transpose(square[...])[0:outs, 0:b_dev]

    all_but_one(res, b_dev, 4).wait_recv()
    correction = mm(gain[...], res[...], NN, HIGHEST)
    change = jnp.concatenate([-own_res, correction], axis=0)
    high = change.astype(jnp.bfloat16)
    rest = change - high.astype(jnp.float32)
    middle = rest.astype(jnp.bfloat16)
    low = (rest - middle.astype(jnp.float32)).astype(jnp.bfloat16)
    change3 = jnp.concatenate([high, middle, low], axis=0)
    pick3 = jnp.concatenate([pick[...]] * 3, axis=0)
    updated[...] = coef[...] + mm(change3, pick3, TN)[0:outs]

    for slot, ref, size in ((0, rows, b_dev), (1, nys, s_dev), (2, eigs, s_dev),
                            (3, part, b_dev), (4, res, b_dev)):
        all_but_one(ref, size, slot).wait_send()


def per_device(n_grp, n_dev, centres, coefficients, targets, batch_index, nys_index, eigvecs, eig_scale):
    n = n_grp * n_dev
    c_dev, feat = centres.shape
    outs = coefficients.shape[0]
    b_dev, s_dev, q = batch_index.shape[0], nys_index.shape[0], eigvecs.shape[1]
    batch, sub = n * b_dev, n * s_dev
    wide_out = -(-outs // 128) * 128
    width = min(512, batch)
    vmem = pl.BlockSpec(memory_space=pltpu.VMEM)
    smem = pl.BlockSpec(memory_space=pltpu.SMEM)
    hbm = pl.BlockSpec(memory_space=pl.ANY)
    f32, bf16 = jnp.float32, jnp.bfloat16
    updated, residual = pl.pallas_call(
        functools.partial(kernel, n_grp, n_dev),
        out_shape=(jax.ShapeDtypeStruct((outs, c_dev), f32), jax.ShapeDtypeStruct((outs, b_dev), f32)),
        in_specs=[smem, smem, vmem, vmem, vmem, hbm, hbm],
        out_specs=(vmem, vmem),
        scratch_shapes=[
            pltpu.VMEM((c_dev, feat), bf16),
            pltpu.VMEM((outs, c_dev), f32),
            pltpu.VMEM((outs, c_dev), bf16),
            pltpu.VMEM((c_dev, 128), f32),
            pltpu.VMEM((batch, feat), bf16),
            pltpu.VMEM((sub, feat), bf16),
            pltpu.VMEM((sub, q), f32),
            pltpu.VMEM((b_dev + s_dev, c_dev), bf16),
            pltpu.VMEM((wide_out, width), f32),
            pltpu.VMEM((batch, wide_out), f32),
            pltpu.VMEM((batch, wide_out), f32),
            pltpu.VMEM((batch, wide_out), f32),
            pltpu.VMEM((s_dev, batch), f32),
            pltpu.VMEM((wide_out, wide_out), f32),
            pltpu.SemaphoreType.DMA((2,)),
            pltpu.SemaphoreType.DMA((5,)),
            pltpu.SemaphoreType.DMA((5,)),
        ],
        compiler_params=pltpu.CompilerParams(
            collective_id=0, has_side_effects=True, vmem_limit_bytes=56 * 1024 * 1024),
    )(batch_index, nys_index, eig_scale.reshape(1, q), targets, eigvecs, centres, coefficients)
    return updated, residual


def solution(mesh):
    both = ("grp", "dev")
    in_specs = (P(both, None), P(None, both), P(None, both), P(both), P(both), P(both, None), P())
    out_specs = (P(None, both), P(None, both))
    return jax.shard_map(
        functools.partial(per_device, mesh.shape["grp"], mesh.shape["dev"]),
        mesh=mesh, in_specs=in_specs, out_specs=out_specs, check_vma=False)
```

time: 232 us -> 58.1 us (0.25)
  waiting for transfers between devices: 123 us -> 0 us
  blocking collectives: 72.9 us -> 0 us
  Pallas kernels: 0 us -> 52.1 us
  matrix products: 13.8 us -> 0 us
  between operations: 14.1 us -> 0.64 us
  other arithmetic: 3.89 us -> 0 us
    psum x1 -> x0, waiting for transfers between devices: 123 us -> none  [per_device(): residual = lax.psum(partial_value, ('grp', 'dev'))]
    all_gather x1 -> x0, blocking collectives: 72.9 us -> none  [per_device(): lax.all_gather(own_rows, ('grp', 'dev'), axis=0, tiled=True)]
    pallas_call x0 -> x1, Pallas kernels: none -> 52.1 us  [per_device(): pl.pallas_call(functools.partial(kernel, n_grp, n_dev), out_shape=(jax.Sh...]
    dot_general x9 -> x0, matrix products: 13.8 us -> none  [the longest x1 4.22 us: score_block(): lax.dot_general(coef_bf, kernel, (((1,), (1,)), ((), ())), preferred_elem...]
    reduce_sum x2 -> x0, other arithmetic: 2.98 us -> none  [the longest x1 2.8 us: kernel_block(): right_sq = jnp.sum(jnp.square(right_rows.astype(jnp.float32)), axis=1)]
    unnamed x20 -> x2, local copies, waits for them, and re-layouts: 0.83 us -> 3.54 us
  transfers between devices with their start and end apart: 1 -> 0, of which waited for: 1 -> 0; matrix products, arithmetic and copies ran while one was open for 0% -> 0% of each run, Pallas kernels for 0% -> 0%
where the time goes in v1:
time: 58.1 us; the launch traced here: 57.7 us
  Pallas kernels  52.1 us (90%)
  local copies, waits for them, and re-layouts  5.02 us (9%)
  between operations  0.64 us (1%)
    pallas_call x1, Pallas kernels, per_device(): pl.pallas_call(functools.partial(kernel, n_grp, n_dev), out_shape=(jax.Sh...  52.1 us
    unnamed x2, local copies, waits for them, and re-layouts  3.54 us
    pallas_call x1, local copies, waits for them, and re-layouts, per_device(): pl.pallas_call(functools.partial(kernel, n_grp, n_dev), out_shape=(jax.Sh...  1.48 us

profile of v1, /device:TPU:0, one launch (start us, length us, event | category | flops | bytes accessed | tf_op | source)
XLA Modules:
  0.0 57.7 jit_solution(12749885072568893783)
XLA Ops:
  0.6 1.4 %copy.9.targets = f32[100,16]{1,0:T(8,128)} copy(f32[100,16]{0,1:T(8,128)} %param.9) | data formatting | bytes 12800 | tf_op args[2]
  2.0 52.1 %shard_map.86 = (f32[100,2048]{1,0:T(8,128)}, f32[100,16]{1,0:T(8,128)}) custom-call(s32[16]{0:T(128)} %bidx.1, s32[16]{0:T(128)} %nidx.1, f32[1,128]{1,0:T(1,128)} %bitcast.1, f32[100,16]{1,0:T(8,128)} %copy.9.targets, f32[16,128]{1,0:T(8,128)} %eig.1, bf16[2048,512]{1,0:T(8,128)(2,1)} %centres_hbm.1, f32[100,2048]{1,0:T(8,128)} %coef_hbm.1), custom_call_target="tpu_custom_call" | custom-call | tf_op jit(solution)/shard_map/pallas_call | solution.py:207
  54.1 1.5 %copy.10 = f32[100,16]{0,1:T(8,128)} copy(f32[100,16]{1,0:T(8,128)} %get-tuple-element.3) | data formatting | bytes 12800 | tf_op jit(solution)/shard_map/pallas_call | solution.py:207
  55.6 2.1 %copy.12 = f32[100,2048]{1,0:T(8,128)} copy(f32[100,2048]{1,0:T(8,128)} %get-tuple-element.6) | data formatting | bytes 1638400

commit v2 on v1

v2 whole, which is shorter than its diff:
```python
import functools
import math

import jax
import jax.numpy as jnp
from jax import lax
from jax.experimental import pallas as pl
from jax.experimental.pallas import tpu as pltpu
from jax.sharding import PartitionSpec as P

MESH = pl.DeviceIdType.MESH
HIGHEST = lax.Precision.HIGHEST
NN = (((1,), (0,)), ((), ()))
NT = (((1,), (1,)), ((), ()))
TN = (((0,), (0,)), ((), ()))


def mm(a, b, dims=NN, precision=None):
    return lax.dot_general(a, b, dims, precision=precision, preferred_element_type=jnp.float32)


def split_square(x):
    f = x.astype(jnp.float32)
    f = f * f
    high = f.astype(jnp.bfloat16)
    low = (f - high.astype(jnp.float32)).astype(jnp.bfloat16)
    return high, low


def square_column(x):
    high, low = split_square(x)
    ones = jnp.ones((x.shape[1], 128), jnp.bfloat16)
    return mm(high, ones) + mm(low, ones)


def square_row(x):
    high, low = split_square(x)
    ones = jnp.ones((8, x.shape[1]), jnp.bfloat16)
    return (mm(ones, high, NT) + mm(ones, low, NT))[0:1]


def laplace(left, left_sq, minus_two_right, right_sq, rate):
    cross = mm(left, minus_two_right, NT)
    wide = jnp.concatenate([left_sq] * (cross.shape[1] // 128), axis=1)
    d2 = jnp.maximum((wide + right_sq) + cross, 1.0)
    return jnp.exp2((d2 * lax.rsqrt(d2)) * rate)


def one_hot(bidx, nidx, c_dev, first):
    b_dev, s_dev = bidx.shape[0], nidx.shape[0]
    total = b_dev + s_dev
    spot = lax.broadcasted_iota(jnp.int32, (total, 128), 0)
    index = jnp.zeros((total, 128), jnp.int32)
    for r in range(b_dev):
        index = jnp.where(spot == r, bidx[r], index)
    for r in range(s_dev):
        index = jnp.where(spot == b_dev + r, nidx[r], index)
    index = jnp.concatenate([index - first] * (c_dev // 128), axis=1)
    hit = lax.broadcasted_iota(jnp.int32, (total, c_dev), 1) == index
    return jnp.where(hit, 1.0, 0.0).astype(jnp.bfloat16)


def kernel(n_grp, n_dev, bidx, nidx, scale, targets, eig, centres_hbm, coef_hbm,
           change,
           centres, coef, coef_bf, csq, rows, nys, eigs, acc, part, pair, summed, got, res, gain, target,
           local_sem, send_sem, recv_sem, pass_send, pass_recv, pair_send, pair_recv, sum_send, sum_recv):
    n = n_grp * n_dev
    grp, dev = lax.axis_index("grp"), lax.axis_index("dev")
    me = grp * n_dev + dev
    c_dev, feat = centres.shape
    outs = coef.shape[0]
    b_dev, s_dev = bidx.shape[0], nidx.shape[0]
    batch, sub = rows.shape[0], nys.shape[0]
    rate = -1.0 / (0.7 * math.sqrt(feat) * math.log(2.0))
    wide_out = part.shape[1]
    band = n_dev * b_dev

    load_centres = pltpu.make_async_copy(centres_hbm, centres, local_sem.at[0])
    load_coef = pltpu.make_async_copy(coef_hbm, coef, local_sem.at[1])
    load_centres.start()
    load_coef.start()

    def chip(k):
        p = lax.rem(dev + k, n_dev)
        return p, {"grp": grp, "dev": p}

    def core(k):
        p = lax.rem(grp + k, n_grp)
        return p, {"grp": p, "dev": dev}

    barrier = pltpu.get_barrier_semaphore()

    @pl.loop(1, n_dev)
    def _(k):
        pl.semaphore_signal(barrier, inc=1, device_id=chip(k)[1], device_id_type=MESH)

    for k in range(1, n_grp):
        pl.semaphore_signal(barrier, inc=1, device_id=core(k)[1], device_id_type=MESH)

    def block(ref, p, size):
        return ref.at[pl.ds(pl.multiple_of(p * size, size), size)]

    def chip_copy(ref, size, slot, k):
        mine = block(ref, me, size)
        return pltpu.make_async_remote_copy(
            src_ref=mine, dst_ref=mine, send_sem=send_sem.at[slot], recv_sem=recv_sem.at[slot, k],
            device_id=chip(k)[1], device_id_type=MESH)

    def pass_on(ref, size, slot, source):
        piece = block(ref, grp * n_dev + source, size)
        for k in range(1, n_grp):
            pltpu.make_async_remote_copy(
                src_ref=piece, dst_ref=piece, send_sem=pass_send.at[slot], recv_sem=pass_recv.at[slot],
                device_id=core(k)[1], device_id_type=MESH).start()

    def gather_start(ref, size, slot):
        @pl.loop(1, n_dev)
        def _(k):
            chip_copy(ref, size, slot, k).start()

        pass_on(ref, size, slot, dev)

    def gather_pass(ref, size, slot):
        @pl.loop(1, n_dev)
        def _(k):
            chip_copy(ref, size, slot, k).wait_recv()
            pass_on(ref, size, slot, lax.rem(dev + n_dev - k, n_dev))

    def many(ref, count, send, recv, where):
        piece = ref.at[pl.ds(0, count)]
        return pltpu.make_async_remote_copy(
            src_ref=piece, dst_ref=piece, send_sem=send, recv_sem=recv, device_id=where, device_id_type=MESH)

    def passed(ref, size, slot):
        return many(ref, (n_grp - 1) * n_dev * size, pass_send.at[slot], pass_recv.at[slot], core(1)[1])

    def gather_sent(ref, size, slot):
        many(ref, (n_dev - 1) * size, send_sem.at[slot], recv_sem.at[slot, 0], chip(1)[1]).wait_send()
        passed(ref, size, slot).wait_send()

    pick = one_hot(bidx, nidx, c_dev, 0)
    block(eigs, me, s_dev)[...] = eig[...]
    pl.semaphore_wait(barrier, (n_dev - 1) + (n_grp - 1))
    gather_start(eigs, s_dev, 2)

    load_centres.wait()
    own = mm(pick, centres[...]).astype(jnp.bfloat16)
    block(rows, me, b_dev)[...] = own[:b_dev]
    block(nys, me, s_dev)[...] = own[b_dev:]
    gather_start(rows, b_dev, 0)
    gather_start(nys, s_dev, 1)

    step = 256 if c_dev % 256 == 0 else 128

    @pl.loop(0, c_dev // step)
    def _(i):
        piece = pl.ds(pl.multiple_of(i * step, step), step)
        csq[piece, :] = square_column(centres[piece, :])

    load_coef.wait()
    coef_bf[...] = coef[...].astype(jnp.bfloat16)
    target[...] = jnp.zeros_like(target)
    target[:, 0:outs] = targets[...]
    acc[...] = jnp.zeros_like(acc)

    width = acc.shape[1]
    gather_pass(rows, b_dev, 0)

    per_band = band // width

    @pl.loop(0, n_grp * per_band)
    def _(j):
        @pl.when(j == per_band)
        def _():
            passed(rows, b_dev, 0).wait_recv()

        first = lax.rem(grp + j // per_band, n_grp) * band + lax.rem(j, per_band) * width
        across = pl.ds(pl.multiple_of(first, width), width)
        piece_rows = rows[across, :]
        bsq = square_row(piece_rows)
        minus_two = piece_rows * jnp.bfloat16(-2.0)
        sums = jnp.zeros((outs, width), jnp.float32)
        for i in range(c_dev // step):
            down = slice(i * step, (i + 1) * step)
            k = laplace(centres[down, :], csq[down, :], minus_two, bsq, rate).astype(jnp.bfloat16)
            sums = sums + mm(coef_bf[:, down], k)
        acc[0:outs, :] = sums
        part[across, :] = jnp.transpose(acc[...])

    for k in range(1, n_grp):
        g, where = core(k)
        pltpu.make_async_remote_copy(
            src_ref=block(part, g, band), dst_ref=pair.at[pl.ds((k - 1) * band, band)],
            send_sem=pair_send, recv_sem=pair_recv, device_id=where, device_id_type=MESH).start()
    pairs = many(pair, (n_grp - 1) * band, pair_send, pair_recv, core(1)[1])
    pairs.wait_recv()
    both = block(part, grp, band)[...]
    for k in range(1, n_grp):
        both = both + pair[(k - 1) * band:k * band, :]
    summed[...] = both

    @pl.loop(1, n_dev)
    def _(k):
        p, where = chip(k)
        pltpu.make_async_remote_copy(
            src_ref=block(summed, p, b_dev), dst_ref=block(got, dev, b_dev),
            send_sem=sum_send, recv_sem=sum_recv, device_id=where, device_id_type=MESH).start()

    block(got, dev, b_dev)[...] = block(summed, dev, b_dev)[...]

    gather_pass(eigs, s_dev, 2)
    gather_pass(nys, s_dev, 1)
    sums_in = many(got, (n_dev - 1) * b_dev, sum_send, sum_recv, chip(1)[1])

    def make_gain():
        passed(eigs, s_dev, 2).wait_recv()
        passed(nys, s_dev, 1).wait_recv()
        weights = mm(eig[...] * scale[...], eigs[...], NT, HIGHEST)
        tall = min(512, sub)
        span = min(512, batch)

        @pl.loop(0, batch // span)
        def _(j):
            across = pl.ds(pl.multiple_of(j * span, span), span)
            piece_rows = rows[across, :]
            bsq = square_row(piece_rows)
            minus_two = piece_rows * jnp.bfloat16(-2.0)
            total_gain = jnp.zeros((s_dev, span), jnp.float32)
            for i in range(sub // tall):
                piece_nys = nys[i * tall:(i + 1) * tall, :]
                kn = laplace(piece_nys, square_column(piece_nys), minus_two, bsq, rate)
                total_gain = total_gain + mm(weights[:, i * tall:(i + 1) * tall], kn, NN, HIGHEST)
            gain[:, across] = total_gain

    sums_in.wait_recv()
    own_res = jnp.sum(got[...].reshape(n_dev, b_dev, wide_out), axis=0) - target[...]
    block(res, me, b_dev)[...] = own_res
    gather_start(res, b_dev, 3)
    change[0:b_dev, :] = own_res
    make_gain()
    gather_pass(res, b_dev, 3)
    passed(res, b_dev, 3).wait_recv()
    change[b_dev:, :] = mm(gain[...], res[...], NN, HIGHEST)

    for slot, ref, size in ((0, rows, b_dev), (1, nys, s_dev), (2, eigs, s_dev), (3, res, b_dev)):
        gather_sent(ref, size, slot)
    pairs.wait_send()
    sums_in.wait_send()


def update_kernel(bidx, nidx, change, coef, updated, res_out):
    outs, width = coef.shape
    b_dev = bidx.shape[0]
    pick = one_hot(bidx, nidx, width, pl.program_id(0) * width)
    own_res = change[0:b_dev, :]
    both = jnp.concatenate([-own_res, change[b_dev:, :]], axis=0)
    high = both.astype(jnp.bfloat16)
    rest = both - high.astype(jnp.float32)
    middle = rest.astype(jnp.bfloat16)
    low = (rest - middle.astype(jnp.float32)).astype(jnp.bfloat16)
    both3 = jnp.concatenate([high, middle, low], axis=0)
    pick3 = jnp.concatenate([pick] * 3, axis=0)
    updated[...] = coef[...] + mm(both3, pick3, TN)[0:outs]
    res_out[...] = own_res[:, 0:outs]


def per_device(n_grp, n_dev, centres, coefficients, targets, batch_index, nys_index, eigvecs, eig_scale):
    n = n_grp * n_dev
    c_dev, feat = centres.shape
    outs = coefficients.shape[0]
    b_dev, s_dev, q = batch_index.shape[0], nys_index.shape[0], eigvecs.shape[1]
    batch, sub, band = n * b_dev, n * s_dev, n_dev * b_dev
    wide_out = -(-outs // 128) * 128
    width = min(512, band)
    vmem = pl.BlockSpec(memory_space=pltpu.VMEM)
    smem = pl.BlockSpec(memory_space=pltpu.SMEM)
    hbm = pl.BlockSpec(memory_space=pl.ANY)
    f32, bf16, dma = jnp.float32, jnp.bfloat16, pltpu.SemaphoreType.DMA
    change = pl.pallas_call(
        functools.partial(kernel, n_grp, n_dev),
        out_shape=jax.ShapeDtypeStruct((b_dev + s_dev, wide_out), f32),
        in_specs=[smem, smem, vmem, vmem, vmem, hbm, hbm],
        out_specs=vmem,
        scratch_shapes=[
            pltpu.VMEM((c_dev, feat), bf16),
            pltpu.VMEM((outs, c_dev), f32),
            pltpu.VMEM((outs, c_dev), bf16),
            pltpu.VMEM((c_dev, 128), f32),
            pltpu.VMEM((batch, feat), bf16),
            pltpu.VMEM((sub, feat), bf16),
            pltpu.VMEM((sub, q), f32),
            pltpu.VMEM((wide_out, width), f32),
            pltpu.VMEM((batch, wide_out), f32),
            pltpu.VMEM(((n_grp - 1) * band, wide_out), f32),
            pltpu.VMEM((band, wide_out), f32),
            pltpu.VMEM((band, wide_out), f32),
            pltpu.VMEM((batch, wide_out), f32),
            pltpu.VMEM((s_dev, batch), f32),
            pltpu.VMEM((b_dev, wide_out), f32),
            dma((2,)), dma((4,)), dma((4, n_dev)), dma((4,)), dma((4,)), dma, dma, dma, dma,
        ],
        compiler_params=pltpu.CompilerParams(
            collective_id=0, has_side_effects=True, vmem_limit_bytes=56 * 1024 * 1024),
    )(batch_index, nys_index, eig_scale.reshape(1, q), targets.T, eigvecs, centres, coefficients)
    columns = 1024 if c_dev % 1024 == 0 else c_dev
    whole = pl.BlockSpec((b_dev + s_dev, wide_out), lambda i: (0, 0))
    tile = pl.BlockSpec((outs, columns), lambda i: (0, i))
    updated, residual = pl.pallas_call(
        update_kernel,
        grid=(c_dev // columns,),
        out_shape=(jax.ShapeDtypeStruct((outs, c_dev), f32), jax.ShapeDtypeStruct((b_dev, outs), f32)),
        in_specs=[smem, smem, whole, tile],
        out_specs=(tile, pl.BlockSpec((b_dev, outs), lambda i: (0, 0))),
    )(batch_index, nys_index, change, coefficients)
    return updated, residual.T


def solution(mesh):
    both = ("grp", "dev")
    in_specs = (P(both, None), P(None, both), P(None, both), P(both), P(both), P(both, None), P())
    out_specs = (P(None, both), P(None, both))
    return jax.shard_map(
        functools.partial(per_device, mesh.shape["grp"], mesh.shape["dev"]),
        mesh=mesh, in_specs=in_specs, out_specs=out_specs, check_vma=False)
```

time: 58.1 us -> 41.1 us (0.71)
  Pallas kernels: 52.1 us -> 40.1 us
  local copies, waits for them, and re-layouts: 5.02 us -> 0 us
    pallas_call x1 -> x2, Pallas kernels: 52.1 us -> 40.1 us  [the longest x1 37.7 us: per_device(): pl.pallas_call(functools.partial(kernel, n_grp, n_dev), out_shape=jax.Sha...]
    unnamed x2 -> x0, local copies, waits for them, and re-layouts: 3.54 us -> none
    pallas_call x1 -> x0, local copies, waits for them, and re-layouts: 1.48 us -> none  [per_device(): pl.pallas_call(functools.partial(kernel, n_grp, n_dev), out_shape=(jax.Sh...]
where the time goes in v2:
time: 41.1 us; the launch traced here: 40.7 us
  Pallas kernels  40.1 us (98%)
  between operations  0.64 us (2%)
    pallas_call x1, Pallas kernels, per_device(): pl.pallas_call(functools.partial(kernel, n_grp, n_dev), out_shape=jax.Sha...  37.7 us
    pallas_call x1, Pallas kernels, per_device(): pl.pallas_call(update_kernel, grid=(c_dev // columns,), out_shape=(jax.Sh...  2.33 us

profile of v2, /device:TPU:0, one launch (start us, length us, event | category | flops | bytes accessed | tf_op | source)
XLA Modules:
  0.0 40.7 jit_solution(11446396813664867453)
XLA Ops:
  0.6 37.7 %shard_map.86.change = f32[32,128]{1,0:T(8,128)} custom-call(s32[16]{0:T(128)} %bidx.3, s32[16]{0:T(128)} %nidx.3, f32[1,128]{1,0:T(1,128)} %bitcast.4, f32[16,100]{1,0:T(8,128)} %bitcast.3, f32[16,128]{1,0:T(8,128)} %eig.1, bf16[2048,512]{1,0:T(8,128)(2,1)} %centres_hbm.1, f32[100,2048]{1,0:T(8,128)} %coef.1), custom_call_target="tpu_custom_call" | custom-call | tf_op jit(solution)/shard_map/pallas_call | solution.py:279
  38.4 2.3 %shard_map.87 = (f32[100,2048]{1,0:T(8,128)}, f32[16,100]{1,0:T(8,128)}) custom-call(s32[16]{0:T(128)} %bidx.3, s32[16]{0:T(128)} %nidx.3, f32[32,128]{1,0:T(8,128)} %shard_map.86.change, f32[100,2048]{1,0:T(8,128)} %coef.1), custom_call_target="tpu_custom_call" | custom-call | tf_op jit(solution)/shard_map/pallas_call | solution.py:308

commit v3 on v2

--- a/solution.py
+++ b/solution.py
@@ -148,7 +148,6 @@
     block(rows, me, b_dev)[...] = own[:b_dev]
     block(nys, me, s_dev)[...] = own[b_dev:]
     gather_start(rows, b_dev, 0)
-    gather_start(nys, s_dev, 1)
 
     step = 256 if c_dev % 256 == 0 else 128
 
@@ -165,6 +164,7 @@
 
     width = acc.shape[1]
     gather_pass(rows, b_dev, 0)
+    gather_start(nys, s_dev, 1)
 
     per_band = band // width
 

time: 41.1 us -> 38.6 us (0.939)
  Pallas kernels: 40.1 us -> 37.6 us
    pallas_call x1, Pallas kernels: 37.7 us -> 35.3 us  [per_device(): pl.pallas_call(functools.partial(kernel, n_grp, n_dev), out_shape=jax.Sha...]
where the time goes in v3:
time: 38.6 us; the launch traced here: 38.3 us
  Pallas kernels  37.6 us (97%)
  between operations  0.64 us (2%)
    pallas_call x1, Pallas kernels, per_device(): pl.pallas_call(functools.partial(kernel, n_grp, n_dev), out_shape=jax.Sha...  35.3 us
    pallas_call x1, Pallas kernels, per_device(): pl.pallas_call(update_kernel, grid=(c_dev // columns,), out_shape=(jax.Sh...  2.33 us

profile of v3, /device:TPU:0, one launch (start us, length us, event | category | flops | bytes accessed | tf_op | source)
XLA Modules:
  0.0 38.3 jit_solution(17587852419591076623)
XLA Ops:
  0.6 35.3 %shard_map.86.change = f32[32,128]{1,0:T(8,128)} custom-call(s32[16]{0:T(128)} %bidx.3, s32[16]{0:T(128)} %nidx.3, f32[1,128]{1,0:T(1,128)} %bitcast.4, f32[16,100]{1,0:T(8,128)} %bitcast.3, f32[16,128]{1,0:T(8,128)} %eig.1, bf16[2048,512]{1,0:T(8,128)(2,1)} %centres_hbm.1, f32[100,2048]{1,0:T(8,128)} %coef.1), custom_call_target="tpu_custom_call" | custom-call | tf_op jit(solution)/shard_map/pallas_call | solution.py:279
  35.9 2.3 %shard_map.87 = (f32[100,2048]{1,0:T(8,128)}, f32[16,100]{1,0:T(8,128)}) custom-call(s32[16]{0:T(128)} %bidx.3, s32[16]{0:T(128)} %nidx.3, f32[32,128]{1,0:T(8,128)} %shard_map.86.change, f32[100,2048]{1,0:T(8,128)} %coef.1), custom_call_target="tpu_custom_call" | custom-call | tf_op jit(solution)/shard_map/pallas_call | solution.py:308

commit v4 on v3

--- a/solution.py
+++ b/solution.py
@@ -208,8 +208,6 @@
 
     block(got, dev, b_dev)[...] = block(summed, dev, b_dev)[...]
 
-    gather_pass(eigs, s_dev, 2)
-    gather_pass(nys, s_dev, 1)
     sums_in = many(got, (n_dev - 1) * b_dev, sum_send, sum_recv, chip(1)[1])
 
     def make_gain():
@@ -237,6 +235,8 @@
     block(res, me, b_dev)[...] = own_res
     gather_start(res, b_dev, 3)
     change[0:b_dev, :] = own_res
+    gather_pass(eigs, s_dev, 2)
+    gather_pass(nys, s_dev, 1)
     make_gain()
     gather_pass(res, b_dev, 3)
     passed(res, b_dev, 3).wait_recv()

time: 38.6 us -> 38.6 us (level)
  no operation moved by 1% of the time
where the time goes in v4:
time: 38.6 us; the launch traced here: 38.3 us
  Pallas kernels  37.6 us (97%)
  between operations  0.64 us (2%)
    pallas_call x1, Pallas kernels, per_device(): pl.pallas_call(functools.partial(kernel, n_grp, n_dev), out_shape=jax.Sha...  35.3 us
    pallas_call x1, Pallas kernels, per_device(): pl.pallas_call(update_kernel, grid=(c_dev // columns,), out_shape=(jax.Sh...  2.33 us

profile of v4, /device:TPU:0, one launch (start us, length us, event | category | flops | bytes accessed | tf_op | source)
XLA Modules:
  0.0 38.3 jit_solution(4519356212798868441)
XLA Ops:
  0.6 35.3 %shard_map.86.change = f32[32,128]{1,0:T(8,128)} custom-call(s32[16]{0:T(128)} %bidx.3, s32[16]{0:T(128)} %nidx.3, f32[1,128]{1,0:T(1,128)} %bitcast.4, f32[16,100]{1,0:T(8,128)} %bitcast.3, f32[16,128]{1,0:T(8,128)} %eig.1, bf16[2048,512]{1,0:T(8,128)(2,1)} %centres_hbm.1, f32[100,2048]{1,0:T(8,128)} %coef.1), custom_call_target="tpu_custom_call" | custom-call | tf_op jit(solution)/shard_map/pallas_call | solution.py:279
  35.9 2.3 %shard_map.87 = (f32[100,2048]{1,0:T(8,128)}, f32[16,100]{1,0:T(8,128)}) custom-call(s32[16]{0:T(128)} %bidx.3, s32[16]{0:T(128)} %nidx.3, f32[32,128]{1,0:T(8,128)} %shard_map.86.change, f32[100,2048]{1,0:T(8,128)} %coef.1), custom_call_target="tpu_custom_call" | custom-call | tf_op jit(solution)/shard_map/pallas_call | solution.py:308
